TPU v7x, 128 devices: a whole 4x4x4 slice. The times are simulated.
128 devices in a mesh: ctx: 32 (over y, z, core), head: 4 (over x).
Axes of the slice: x: 4, y: 4, z: 4, core: 2. Of those that a mesh axis runs over, the one named last changes fastest.
Arguments:
- queries: bfloat16 [65536, 2048], P('ctx', 'head'), may hold values from -8 to 6
- key_input: bfloat16 [65536, 2048], P('ctx', 'head'), may hold values from -8 to 6
- value_input: bfloat16 [65536, 2048], P('ctx', 'head'), may hold values from -6 to 6
- out_weight: bfloat16 [2048, 2048], P('head'), may hold values from -0.125 to 0.125
- cotangent: bfloat16 [65536, 2048], P('ctx', 'head'), may hold values from -6 to 6
Outputs:
- layer_out: bfloat16 [65536, 2048], P('ctx', 'head')
- grad_query: bfloat16 [65536, 2048], P('ctx', 'head')
- grad_key: bfloat16 [65536, 2048], P('ctx', 'head')
- grad_value: bfloat16 [65536, 2048], P('ctx', 'head')
All inputs are finite; a program needn't handle non-finite values.
Results may differ from a plain program's by a relative error of at most 0.009.
Values may be sent and summed in bfloat16 or wider, within the bound.
No kernel may reach another device: no remote copies, remote signals or barrier semaphores. Data moves between devices by JAX's collectives and lax.ppermute only.
A program may use at most 192 MiB of HBM per device.

v0:
```python
import jax
import jax.numpy as jnp
from jax import lax
from jax.sharding import PartitionSpec as P

DH = 128
BLOCK = 512


HIGH = lax.Precision.HIGHEST


def entering(part, axis, combine, identity, reverse):
    count = lax.axis_size(axis)
    place = lax.axis_index(axis)
    ahead = count - 1 - place if reverse else place
    gathered = jax.tree.map(lambda a: lax.all_gather(a, axis), part)
    state = jax.tree.map(lambda a, e: jnp.zeros_like(a) + jnp.asarray(e, a.dtype), part, identity)

    def one(step, state):
        source = count - 1 - step if reverse else step
        return combine(
            state, jax.tree.map(lambda a: lax.dynamic_index_in_dim(a, source, 0, False), gathered)
        )

    return lax.fori_loop(0, ahead, one, state)


def feature(inputs):
    lifted = inputs.astype(jnp.float32)
    return jnp.where(lifted > 0, lifted + 1.0, jnp.exp(jnp.minimum(lifted, 0.0)))


def slope(inputs):
    lifted = inputs.astype(jnp.float32)
    return jnp.where(lifted > 0, 1.0, jnp.exp(jnp.minimum(lifted, 0.0)))


def add_states(earlier, later):
    return (earlier[0] + later[0], earlier[1] + later[1])


def exclusive_blocks(terms):
    return jnp.concatenate([jnp.zeros_like(terms[:1]), jnp.cumsum(terms, 0)[:-1]], 0)


def exclusive_after(terms):
    return jnp.flip(exclusive_blocks(jnp.flip(terms, 0)), 0)


def split_einsum(form, state, operand, state_first):
    upper = state.astype(jnp.bfloat16)
    rest = (state - upper.astype(jnp.float32)).astype(jnp.bfloat16)
    if state_first:
        return jnp.einsum(form, upper, operand, preferred_element_type=jnp.float32) + jnp.einsum(
            form, rest, operand, preferred_element_type=jnp.float32
        )
    return jnp.einsum(form, operand, upper, preferred_element_type=jnp.float32) + jnp.einsum(
        form, operand, rest, preferred_element_type=jnp.float32
    )


def on_device(queries, key_input, value_input, out_weight, cotangent):
    token_count, width = queries.shape
    head_count = width // DH
    blocks = token_count // BLOCK
    shape4 = (blocks, BLOCK, head_count, DH)
    feat_q = feature(queries).astype(jnp.bfloat16).reshape(shape4)
    feat_k = feature(key_input).astype(jnp.bfloat16).reshape(shape4)
    value_blocks = value_input.reshape(shape4)
    lower = lax.broadcasted_iota(jnp.int32, (BLOCK, BLOCK), 0) >= lax.broadcasted_iota(
        jnp.int32, (BLOCK, BLOCK), 1
    )
    zero_kv = jnp.zeros((head_count, DH, DH), jnp.float32)
    zero_z = jnp.zeros((head_count, DH), jnp.float32)
    block_kv = jnp.einsum(
        "nshd,nshe->nhde", feat_k, value_blocks, preferred_element_type=jnp.float32
    )
    block_z = jnp.sum(feat_k, axis=1, dtype=jnp.float32)
    total_kv = jnp.sum(block_kv, 0)
    total_z = jnp.sum(block_z, 0)
    prior_kv, prior_z = entering((total_kv, total_z), "ctx", add_states, (zero_kv, zero_z), False)
    state_kv = prior_kv[None] + exclusive_blocks(block_kv)
    state_z = prior_z[None] + exclusive_blocks(block_z)
    scores = jnp.einsum("nthd,nshd->nhts", feat_q, feat_k, preferred_element_type=jnp.float32)
    masked = jnp.where(lower, scores, 0.0)
    weights = masked.astype(jnp.bfloat16)
    query_wide = feat_q.astype(jnp.float32)
    numer = jnp.einsum("nhts,nshd->nthd", weights, value_blocks, preferred_element_type=jnp.float32)
    numer = numer + split_einsum("nthd,nhde->nthe", state_kv, feat_q, False)
    denom = jnp.swapaxes(jnp.sum(masked, -1), 1, 2) + jnp.einsum(
        "nthd,nhd->nth", query_wide, state_z, precision=HIGH
    )
    attend = numer / denom[..., None]
    attn_rows = attend.astype(jnp.bfloat16).reshape(token_count, width)
    partial_out = jnp.dot(attn_rows, out_weight, preferred_element_type=jnp.float32)
    layer_out = lax.psum_scatter(partial_out, "head", scatter_dimension=1, tiled=True).astype(
        jnp.bfloat16
    )
    grad_attn = jnp.einsum(
        "tc,wc->tw",
        lax.all_gather(cotangent, "head", axis=1, tiled=True),
        out_weight,
        preferred_element_type=jnp.float32,
    ).reshape(shape4)
    grad_num = (grad_attn / denom[..., None]).astype(jnp.bfloat16)
    grad_den = -jnp.sum(grad_attn * attend, -1) / denom
    block_back_kv = jnp.einsum(
        "nthd,nthe->nhde", feat_q, grad_num, preferred_element_type=jnp.float32
    )
    block_back_z = jnp.einsum("nthd,nth->nhd", query_wide, grad_den, precision=HIGH)
    back_total_kv = jnp.sum(block_back_kv, 0)
    back_total_z = jnp.sum(block_back_z, 0)
    later_kv, later_z = entering(
        (back_total_kv, back_total_z), "ctx", add_states, (zero_kv, zero_z), True
    )
    back_kv = later_kv[None] + exclusive_after(block_back_kv)
    back_z = later_z[None] + exclusive_after(block_back_z)
    grad_score = jnp.einsum(
        "nthe,nshe->nhts", grad_num, value_blocks, preferred_element_type=jnp.float32
    )
    grad_score = grad_score + jnp.swapaxes(grad_den, 1, 2)[..., None]
    grad_weight = jnp.where(lower, grad_score, 0.0).astype(jnp.bfloat16)
    grad_q = jnp.einsum("nhts,nshd->nthd", grad_weight, feat_k, preferred_element_type=jnp.float32)
    grad_q = (
        grad_q
        + split_einsum("nhde,nthe->nthd", state_kv, grad_num, True)
        + grad_den[..., None] * state_z[:, None]
    )
    grad_k = jnp.einsum("nhts,nthd->nshd", grad_weight, feat_q, preferred_element_type=jnp.float32)
    grad_k = grad_k + split_einsum("nhde,nshe->nshd", back_kv, value_blocks, True) + back_z[:, None]
    grad_v = jnp.einsum("nhts,nthe->nshe", weights, grad_num, preferred_element_type=jnp.float32)
    grad_v = grad_v + split_einsum("nhde,nshd->nshe", back_kv, feat_k, True)
    grad_query = (grad_q.reshape(token_count, width) * slope(queries)).astype(jnp.bfloat16)
    grad_key = (grad_k.reshape(token_count, width) * slope(key_input)).astype(jnp.bfloat16)
    grad_value = grad_v.reshape(token_count, width).astype(jnp.bfloat16)
    return (layer_out, grad_query, grad_key, grad_value)


def solution(mesh):
    in_specs = (
        P("ctx", "head"),
        P("ctx", "head"),
        P("ctx", "head"),
        P("head", None),
        P("ctx", "head"),
    )
    out_specs = (P("ctx", "head"), P("ctx", "head"), P("ctx", "head"), P("ctx", "head"))
    return jax.shard_map(
        on_device, mesh=mesh, in_specs=in_specs, out_specs=out_specs, check_vma=False
    )
```

profile of v0, /device:TPU:1, one launch (start us, length us, event | category | flops | bytes accessed | tf_op | source)
XLA Modules:
  0.0 409.7 jit_solution(11893390444670694735)
XLA Ops:
  8.0 4.0 reshape.44
  11.9 4.1 convert_reduce_fusion.1
  16.0 4.0 reshape.43
  19.9 4.3 %copy.79 = bf16[4,512,4,128]{1,3,2,0:T(8,128)(2,1)} copy(bf16[4,512,4,128]{3,2,1,0:T(4,128)(2,1)} %reshape.43) | data formatting | bytes 4194304 | tf_op jit(solution)/shard_map/reshape | solution.py:69
  24.3 4.0 fusion.47
  28.3 4.0 fusion.1
  32.4 4.0 reshape.42
  36.3 4.3 %copy.98 = bf16[4,512,4,128]{1,3,2,0:T(8,128)(2,1)} copy(bf16[4,512,4,128]{3,2,1,0:T(4,128)(2,1)} %reshape.42) | data formatting | bytes 4194304 | tf_op jit(solution)/shard_map/reshape | solution.py:68
  40.6 2.6 convert_reduce_fusion
  44.0 27.0 %all_gather.30 = f32[32,4,128]{2,1,0:T(4,128)S(1)} all-gather(f32[1,4,128]{2,1,0:T(4,128)S(1)} %bitcast.119), channel_id=1, replica_groups=mesh['ctx'=32,'head'=4] {'ctx'}, dimensions={0}, use_global_device_ids=true | all-gather | bytes 67584 | tf_op jit(solution)/shard_map/all_gather | solution.py:17
  71.2 2.8 select_reduce_fusion
  74.0 3.2 copy-done.25
  77.2 3.6 fusion.16
  80.8 15.1 %all-gather.8.cloned.1.call-done = bf16[2048,2048]{1,0:T(8,128)(2,1)} async-done(((bf16[2048,512]{1,0:T(8,128)(2,1)}), bf16[2048,2048]{1,0:T(8,128)(2,1)}) %all-gather.8.cloned.1.call-update) | async-done | bytes 8388624 | tf_op jit(solution)/shard_map/all_gather | solution.py:102
  96.0 9.6 %fusion.54 = f32[2048,512]{1,0:T(8,128)} fusion(bf16[2048,2048]{1,0:T(8,128)(2,1)} %all-gather.8.cloned.1.call-done, bf16[512,2048]{1,0:T(8,128)(2,1)S(1)} %copy-done), kind=kOutput, calls=%fused_computation.83 | convolution fusion | flops 4294967296 | bytes 14680064 | tf_op jit(solution)/shard_map/tc,wc->tw/dot_general | solution.py:100
  105.6 5.3 %reshape.46 = f32[4,512,4,128]{3,2,1,0:T(4,128)} reshape(f32[2048,512]{1,0:T(8,128)} %fusion.54) | data formatting | bytes 8388608 | tf_op jit(solution)/shard_map/reshape | solution.py:105
  110.9 5.3 %copy.86 = f32[4,512,4,128]{1,3,2,0:T(8,128)} copy(f32[4,512,4,128]{3,2,1,0:T(4,128)} %reshape.46) | data formatting | bytes 8388608 | tf_op jit(solution)/shard_map/reshape | solution.py:105
  116.2 36.6 %all-gather.10.cloned.1.call-done = f32[128,128,128]{2,1,0:T(8,128)} async-done(((f32[4,128,128]{2,1,0:T(8,128)}), f32[128,128,128]{2,1,0:T(8,128)}) %all-gather.10.cloned.1.call-update) | async-done | bytes 8388624 | tf_op jit(solution)/shard_map/all_gather | solution.py:17
  152.8 1.2 while.26
  154.0 2.5 fusion.53
  156.6 2.5 fusion.36
  160.0 4.3 %multiply_reduce_fusion = (f32[4,512,4]{1,2,0:T(4,128)S(1)}, bf16[4,512,4,128]{1,3,2,0:T(8,128)(2,1)}, bf16[4,512,4,128]{1,3,2,0:T(8,128)(2,1)S(1)}) fusion(f32[4,512,4,128]{1,3,2,0:T(8,128)S(1)} %copy-done.18, f32[4,512,4]{1,2,0:T(4,128)S(1)} %fusion.40, f32[4,4,128,512]{3,2,1,0:T(8,128)S(1)} %fusion.36, bf16[4,512,4,128]{1,3,2,0:T(8,128)(2,1)S(1)} %copy-done.3, ...), kind=kOutput, calls=%fused_computation.32 | convolution fusion | flops 278126592 | bytes 19988480 | tf_op jit(solution)/shard_map/nthd,nhde->nthe/dot_general | solution.py:58
  164.4 2.4 fusion.48
  166.8 4.2 %copy.85 = bf16[4,512,4,128]{3,2,1,0:T(4,128)(2,1)} copy(bf16[4,512,4,128]{1,3,2,0:T(8,128)(2,1)} %get-tuple-element.150) | data formatting | bytes 4194304 | tf_op jit(solution)/shard_map/convert_element_type | solution.py:95
  171.1 9.6 %fusion.17 = f32[2048,2048]{1,0:T(8,128)} fusion(bf16[512,2048]{1,0:T(8,128)(2,1)S(1)} %copy-done, bf16[256,8,4,128]{3,2,1,0:T(4,128)(2,1)} %bitcast.109), kind=kOutput, calls=%fused_computation.39 | convolution fusion | flops 4294967296 | bytes 20971520 | tf_op jit(solution)/shard_map/dot_general | solution.py:96
  180.7 1.5 copy-done.4
  182.3 1.7 fusion.38
  184.6 2.3 rev.14
  186.9 1.5 fusion.51
  189.1 2.6 fusion.34
  191.7 2.8 fusion.45
  194.5 3.8 select_convert_fusion
  198.3 3.2 copy-done.10
  201.5 5.8 %fusion.13 = f32[4,512,4,128]{1,3,2,0:T(8,128)} fusion(f32[4,4,512,128]{2,3,1,0:T(8,128)S(1)} %copy-done.16, f32[4,4,512,128]{2,3,1,0:T(8,128)} %fusion.45, bf16[4,512,4,128]{1,3,2,0:T(8,128)(2,1)S(1)} %copy-done.14, bf16[4,4,512,512]{2,3,1,0:T(8,128)(2,1)S(1)} %select_convert_fusion, f32[4,4,128]{2,1,0:T(4,128)S(1)} %pad_add_fusion.1, ...), kind=kOutput, calls=%fused_computation.28 | convolution fusion | flops 1077936128 | bytes 23109632 | tf_op jit(solution)/shard_map/nhts,nshd->nthd/dot_general | solution.py:124
  207.3 5.3 %copy.97 = f32[4,512,4,128]{3,2,1,0:T(4,128)} copy(f32[4,512,4,128]{1,3,2,0:T(8,128)} %fusion.13) | data formatting | bytes 8388608 | tf_op jit(solution)/shard_map/add | solution.py:126
  212.7 1.1 concatenate.14
  213.7 53.9 %all-gather.3 = f32[32,4,128]{2,1,0:T(4,128)S(1)} all-gather(f32[1,4,128]{2,1,0:T(4,128)S(1)} %bitcast.120), channel_id=4, replica_groups=mesh['ctx'=32,'head'=4] {'ctx'}, dimensions={0}, use_global_device_ids=true | all-gather | bytes 67584 | tf_op jit(solution)/shard_map/all_gather | solution.py:17
  267.6 8.5 %fusion.55 = f32[4,4,128,512]{3,2,1,0:T(8,128)} fusion(bf16[4,512,4,128]{1,3,2,0:T(8,128)(2,1)S(1)} %copy-done.4, bf16[4,4,512,512]{2,3,1,0:T(8,128)(2,1)} %copy-done.10), kind=kOutput, calls=%fused_computation.84 | convolution fusion | flops 1073741824 | bytes 14680064 | tf_op jit(solution)/shard_map/nhts,nthd->nshd/dot_general | solution.py:130
  276.1 8.3 %fusion.15 = f32[4,4,128,512]{3,2,1,0:T(8,128)} fusion(bf16[4,512,4,128]{1,3,2,0:T(8,128)(2,1)S(1)} %copy-done.13, bf16[4,4,512,512]{2,3,1,0:T(8,128)(2,1)} %copy-done.25, pred[512,512]{0,1:T(8,128)(4,1)S(1)} %copy-done.21), kind=kOutput, calls=%fused_computation.36 | convolution fusion | flops 1077936128 | bytes 14942208 | tf_op jit(solution)/shard_map/nhts,nthe->nshe/dot_general | solution.py:132
  284.5 31.9 %while.27 = (s32[]{:T(128)}, f32[4,128,128]{2,1,0:T(8,128)S(1)}, f32[4,128]{1,0:T(4,128)S(1)}, s32[]{:T(128)}, f32[32,4,128,128]{3,2,1,0:T(8,128)}, /*index=5*/f...) while((s32[]{:T(128)}, f32[4,128,128]{2,1,0:T(8,128)S(1)}, ...), condition=%wide.region_13.14_spmd, body=%wide.region_12.13_spmd.sunk | while | flops 66054 | bytes 792739 | solution.py:26
  284.5 1.1 bitcast_add_fusion.14
  288.9 1.0 bitcast_add_fusion.14
  290.0 1.0 bitcast_add_fusion.14
  292.1 1.0 bitcast_add_fusion.14
  293.2 1.0 bitcast_add_fusion.14
  295.3 1.0 bitcast_add_fusion.14
  297.4 1.0 bitcast_add_fusion.14
  298.5 1.0 bitcast_add_fusion.14
  300.6 1.0 bitcast_add_fusion.14
  303.8 1.0 bitcast_add_fusion.14
  305.9 1.0 bitcast_add_fusion.14
  309.0 1.0 bitcast_add_fusion.14
  312.2 1.0 bitcast_add_fusion.14
  314.3 1.0 bitcast_add_fusion.14
  316.4 1.7 subtract_convert_fusion
  319.0 2.3 fusion.12
  321.3 4.4 %copy.110 = bf16[4,512,4,128]{3,2,1,0:T(4,128)(2,1)} copy(bf16[4,512,4,128]{1,3,2,0:T(8,128)(2,1)} %fusion.12) | data formatting | bytes 4194304 | tf_op jit(solution)/shard_map/convert_element_type | solution.py:136
  325.7 3.4 copy.168
  329.9 1.5 copy-done.15
  331.4 2.9 add_bitcast_fusion
  334.3 5.3 %copy.104 = f32[4,512,4,128]{3,2,1,0:T(4,128)} copy(f32[4,512,4,128]{1,3,2,0:T(8,128)} %add_bitcast_fusion) | data formatting | bytes 8388608 | tf_op jit(solution)/shard_map/add | solution.py:131
  339.7 8.1 %fusion.5 = (bf16[2048,512]{1,0:T(8,128)(2,1)}, bf16[2048,512]{1,0:T(8,128)(2,1)}) fusion(bf16[2048,512]{1,0:T(8,128)(2,1)} %param.9, f32[256,8,4,128]{3,2,1,0:T(4,128)} %bitcast.105, bf16[2048,512]{1,0:T(8,128)(2,1)} %param.10, f32[256,8,4,128]{3,2,1,0:T(4,128)} %bitcast.106), kind=kLoop, calls=%fused_computation.18 | loop fusion | flops 12582912 | bytes 16777216 | tf_op jit(solution)/shard_map/convert_element_type | solution.py:134
  347.7 51.7 %reduce-scatter.2.cloned.1.call-done = f32[2048,512]{1,0:T(8,128)} async-done(((f32[2048,2048]{1,0:T(8,128)}), f32[2048,512]{1,0:T(8,128)}) %reduce-scatter.2.cloned.1.call-update) | async-done | bytes 4194320 | tf_op jit(solution)/shard_map/reduce_scatter | solution.py:97
  399.4 3.8 convert_element_type.83
  (130 shorter events, 23.5 us)
Async XLA Ops:
  7.2 88.8 %copy-start = (bf16[512,2048]{1,0:T(8,128)(2,1)S(1)}, bf16[512,2048]{1,0:T(8,128)(2,1)}, u32[]{:S(2)}) copy-start(bf16[512,2048]{1,0:T(8,128)(2,1)} %param.12) | copy-start | bytes 6291460
  7.2 88.8 %all-gather.8.cloned.1.call-start = ((), (), s32[]{:S(2)}) async-start(), calls=%async_computation.2 | async-start | bytes 10485760 | tf_op jit(solution)/shard_map/all_gather | solution.py:102
  7.9 144.8 %all-gather.10.cloned.1.call-start = ((), (), s32[]{:S(2)}) async-start(), calls=%async_computation.3 | async-start | bytes 8650752 | tf_op jit(solution)/shard_map/all_gather | solution.py:17
  28.3 256.2 %all-gather.12.cloned.1.call-start = ((), (), s32[]{:S(2)}) async-start(), calls=%async_computation.4 | async-start | bytes 8650752 | tf_op jit(solution)/shard_map/all_gather | solution.py:17
  40.6 30.5 %copy-start.2 = (bf16[4,512,4,128]{1,3,2,0:T(8,128)(2,1)S(1)}, bf16[4,512,4,128]{1,3,2,0:T(8,128)(2,1)}, u32[]{:S(2)}) copy-start(bf16[4,512,4,128]{1,3,2,0:T(8,128)(2,1)} %copy.98) | copy-start | bytes 6291460
  40.6 30.5 %copy-start.5 = (bf16[4,512,4,128]{3,2,1,0:T(4,128)(2,1)S(1)}, bf16[4,512,4,128]{3,2,1,0:T(4,128)(2,1)}, u32[]{:S(2)}) copy-start(bf16[4,512,4,128]{3,2,1,0:T(4,128)(2,1)} %reshape.43) | copy-start | bytes 6291460
  43.2 30.8 %copy-start.22 = (f32[4,4,128]{2,1,0:T(4,128)}, f32[4,4,128]{2,1,0:T(4,128)S(1)}, u32[]{:S(2)}) copy-start(f32[4,4,128]{2,1,0:T(4,128)S(1)} %fusion.50) | copy-start | bytes 24580
  71.1 2.9 copy-start.20
  71.1 6.1 %copy-start.7 = (bf16[4,512,4,128]{3,2,1,0:T(4,128)(2,1)S(1)}, bf16[4,512,4,128]{3,2,1,0:T(4,128)(2,1)}, u32[]{:S(2)}) copy-start(bf16[4,512,4,128]{3,2,1,0:T(4,128)(2,1)} %reshape.44) | copy-start | bytes 6291460
  74.0 3.2 copy-start.25
  116.2 37.8 %slice-start.1 = ((f32[4,4,128]{2,1,0:T(4,128)}), f32[3,4,128]{2,1,0:T(4,128)S(1)}, s32[]{:S(2)}) async-start(f32[4,4,128]{2,1,0:T(4,128)} %copy-done.22), calls=%async_computation.6 | async-start | bytes 12288 | tf_op jit(solution)/shard_map/slice | solution.py:44
  156.5 2.5 copy-start.3
  156.5 3.5 copy-start.18
  164.4 2.4 copy-start.11
  166.8 232.6 %reduce-scatter.2.cloned.1.call-start = ((), (), s32[]{:S(2)}) async-start(), calls=%async_computation.1 | async-start | bytes 20971520 | tf_op jit(solution)/shard_map/reduce_scatter | solution.py:97
  180.7 1.6 copy-start.4
  184.6 7.1 %copy-start.23 = (f32[4,4,128]{2,1,0:T(4,128)}, f32[4,4,128]{2,1,0:T(4,128)S(1)}, u32[]{:S(2)}) copy-start(f32[4,4,128]{2,1,0:T(4,128)S(1)} %fusion.52) | copy-start | bytes 24580
  186.9 2.2 copy-start.12
  188.3 3.3 copy-start.19
  191.7 2.8 copy-start.8
  194.4 7.0 %copy-start.14 = (bf16[4,512,4,128]{1,3,2,0:T(8,128)(2,1)S(1)}, bf16[4,512,4,128]{1,3,2,0:T(8,128)(2,1)}, u32[]{:S(2)}) copy-start(bf16[4,512,4,128]{1,3,2,0:T(8,128)(2,1)} %copy.79) | copy-start | bytes 6291460
  194.4 7.0 %copy-start.16 = (f32[4,4,512,128]{2,3,1,0:T(8,128)S(1)}, f32[4,4,512,128]{2,3,1,0:T(8,128)}, u32[]{:S(2)}) copy-start(f32[4,4,512,128]{2,3,1,0:T(8,128)} %fusion.34) | copy-start | bytes 12582916
  198.3 3.2 copy-start.10
  207.3 5.3 %slice-start.2 = ((f32[4,4,128]{2,1,0:T(4,128)}), f32[3,4,128]{2,1,0:T(4,128)S(1)}, s32[]{:S(2)}) async-start(f32[4,4,128]{2,1,0:T(4,128)} %copy-done.23), calls=%async_computation.7 | async-start | bytes 12288 | tf_op jit(solution)/shard_map/slice | solution.py:44
  207.3 5.3 %slice-start = ((f32[4,4,128,128]{3,2,1,0:T(8,128)}), f32[3,4,128,128]{3,2,1,0:T(8,128)S(1)}, s32[]{:S(2)}) async-start(f32[4,4,128,128]{3,2,1,0:T(8,128)} %copy-done.19), calls=%async_computation.5 | async-start | bytes 1572864 | tf_op jit(solution)/shard_map/slice | solution.py:44
  207.3 6.4 %copy-start.24 = (f32[4,128]{1,0:T(4,128)S(1)}, f32[4,128]{1,0:T(4,128)}, u32[]{:S(2)}) copy-start(f32[4,128]{1,0:T(4,128)} %reduce_sum.69) | copy-start | bytes 6148
  267.6 8.5 %copy-start.13 = (bf16[4,512,4,128]{1,3,2,0:T(8,128)(2,1)S(1)}, bf16[4,512,4,128]{1,3,2,0:T(8,128)(2,1)}, u32[]{:S(2)}) copy-start(bf16[4,512,4,128]{1,3,2,0:T(8,128)(2,1)} %copy-done.11) | copy-start | bytes 6291460
  267.6 8.5 %copy-start.21 = (pred[512,512]{0,1:T(8,128)(4,1)S(1)}, pred[512,512]{0,1:T(8,128)(4,1)}, u32[]{:S(2)}) copy-start(pred[512,512]{0,1:T(8,128)(4,1)} %copy-done.20) | copy-start | bytes 786436
  284.5 33.6 %copy-start.6 = (bf16[4,512,4,128]{3,2,1,0:T(4,128)(2,1)S(1)}, bf16[4,512,4,128]{3,2,1,0:T(4,128)(2,1)}, u32[]{:S(2)}) copy-start(bf16[4,512,4,128]{3,2,1,0:T(4,128)(2,1)} %reshape.43) | copy-start | bytes 6291460
  316.4 2.6 copy-start.17
  321.3 7.9 %copy-start.9 = (bf16[4,512,4,128]{3,2,1,0:T(4,128)(2,1)S(1)}, bf16[4,512,4,128]{3,2,1,0:T(4,128)(2,1)}, u32[]{:S(2)}) copy-start(bf16[4,512,4,128]{3,2,1,0:T(4,128)(2,1)} %reshape.44) | copy-start | bytes 6291460
  329.2 2.2 copy-start.15
  339.7 63.5 %copy-start.1 = (bf16[512,2048]{1,0:T(8,128)(2,1)S(1)}, bf16[512,2048]{1,0:T(8,128)(2,1)}, u32[]{:S(2)}) copy-start(bf16[512,2048]{1,0:T(8,128)(2,1)} %param.12) | copy-start | bytes 6291460
Sparse Core Ops, SparseCore 0:
  9.7 86.2 all-gather.7
  98.2 54.4 all-gather.9
  166.9 83.1 all-gather.11
  252.4 146.9 reduce-scatter.1
where the time goes:
time: 412 us; the launch traced here: 410 us
  waiting for transfers between devices  104 us (25%)
  matrix products  81.7 us (20%)
  blocking collectives  80.9 us (20%)
  local copies, waits for them, and re-layouts  67.9 us (16%)
  other arithmetic  59.9 us (15%)
  between operations  14.1 us (3%)
    all_gather x2, blocking collectives, entering(): gathered = jax.tree.map(lambda a: lax.all_gather(a, axis), part)  80.9 us
    reduce_scatter x1, waiting for transfers between devices, on_device(): lax.psum_scatter(partial_out, 'head', scatter_dimension=1, tiled=True)  51.7 us
    all_gather x2, waiting for transfers between devices, entering(): gathered = jax.tree.map(lambda a: lax.all_gather(a, axis), part)  36.6 us
    add x62, other arithmetic, add_states(): return (earlier[0] + later[0], earlier[1] + later[1])  32.1 us
    all_gather x1, waiting for transfers between devices, on_device(): lax.all_gather(cotangent, 'head', axis=1, tiled=True)  15.1 us
    unnamed x53, local copies, waits for them, and re-layouts  14.1 us
    reshape x2, local copies, waits for them, and re-layouts, on_device(): grad_attn = jnp.einsum('tc,wc->tw', lax.all_gather(cotangent, 'head', axi...  10.6 us
    dot_general x1, matrix products, on_device(): jnp.dot(attn_rows, out_weight, preferred_element_type=jnp.float32)  9.63 us
  transfers between devices with their start and end apart: 4, of which 3 were waited for; matrix products, arithmetic and copies ran while one was open for 44% of the time, Pallas kernels for 0%

commit v1 on v0

v1 whole, which is shorter than its diff:
```python
import functools

import jax
import jax.numpy as jnp
from jax import lax
from jax.experimental import pallas as pl
from jax.experimental.pallas import tpu as pltpu
from jax.sharding import PartitionSpec as P

DH = 128
BLOCK = 512
HALF = BLOCK // 2
NH = 4
NB = 4
ROWS = DH + 8
BF = jnp.bfloat16
F32 = jnp.float32

PARAMS = pltpu.CompilerParams(vmem_limit_bytes=56 * 1024 * 1024)

NN = (((1,), (0,)), ((), ()))
NT = (((1,), (1,)), ((), ()))
TN = (((0,), (0,)), ((), ()))


def dot(a, b, dims):
    return lax.dot_general(a, b, dims, preferred_element_type=F32)


def feature(lifted):
    return jnp.where(lifted > 0, lifted + 1.0, jnp.exp(jnp.minimum(lifted, 0.0)))


def slope(lifted):
    return jnp.where(lifted > 0, 1.0, jnp.exp(jnp.minimum(lifted, 0.0)))


def halves(state):
    upper = state.astype(BF)
    return upper, (state - upper.astype(F32)).astype(BF)


def cols(head):
    return slice(head * DH, (head + 1) * DH)


def totals_kernel(k_ref, v_ref, loc_ref, tot_ref):
    @pl.when(pl.program_id(0) == 0)
    def _():
        tot_ref[...] = jnp.zeros_like(tot_ref)

    for head in range(NH):
        feat = feature(k_ref[:, cols(head)].astype(F32)).astype(BF)
        kv = dot(v_ref[:, cols(head)], feat, TN)
        z = jnp.sum(feat.astype(F32), axis=0, keepdims=True)
        before = tot_ref[head]
        loc_ref[0, head] = before
        tot_ref[head, :DH] = before[:DH] + kv
        tot_ref[head, DH:] = before[DH:] + jnp.broadcast_to(z, (ROWS - DH, DH))


def totals(k, v):
    block = pl.BlockSpec((BLOCK, NH * DH), lambda b: (b, 0))
    return pl.pallas_call(
        totals_kernel,
        grid=(NB,),
        in_specs=[block, block],
        out_specs=[
            pl.BlockSpec((1, NH, ROWS, DH), lambda b: (b, 0, 0, 0)),
            pl.BlockSpec((NH, ROWS, DH), lambda b: (0, 0, 0)),
        ],
        out_shape=[
            jax.ShapeDtypeStruct((NB, NH, ROWS, DH), F32),
            jax.ShapeDtypeStruct((NH, ROWS, DH), F32),
        ],
        compiler_params=PARAMS,
        name="totals",
    )(k, v)


def causal():
    return lax.broadcasted_iota(jnp.int32, (HALF, HALF), 0) >= lax.broadcasted_iota(
        jnp.int32, (HALF, HALF), 1
    )


def attend_kernel(q0, q1, k0, k1, v0, v1, loc_ref, prior_ref, a0, a1, r0, r1):
    lower = causal()
    ones = jnp.ones((BLOCK, DH), BF)
    for block, (q_ref, k_ref, v_ref, a_ref, r_ref) in enumerate(
        ((q0, k0, v0, a0, r0), (q1, k1, v1, a1, r1))
    ):
        fq = feature(q_ref[...].astype(F32)).astype(BF)
        fk = feature(k_ref[...].astype(F32)).astype(BF)
        wide = jnp.concatenate([v_ref[...], ones], axis=1)
        state = prior_ref[0] + loc_ref[block, 0]
        both = jnp.concatenate(
            [state[:DH], jnp.broadcast_to(state[DH : DH + 1], (DH, DH))], axis=0
        )
        sums = jnp.concatenate(halves(both), axis=1)
        past = dot(jnp.concatenate([fq, fq], axis=1), sums, NT)
        w00 = jnp.where(lower, dot(fq[:HALF], fk[:HALF], NT), 0.0).astype(BF)
        w10 = dot(fq[HALF:], fk[:HALF], NT).astype(BF)
        w11 = jnp.where(lower, dot(fq[HALF:], fk[HALF:], NT), 0.0).astype(BF)
        top = past[:HALF] + dot(w00, wide[:HALF], NN)
        low = past[HALF:] + dot(jnp.concatenate([w10, w11], axis=1), wide, NN)
        for rows, res in ((slice(0, HALF), top), (slice(HALF, BLOCK), low)):
            inv = 1.0 / res[:, DH:]
            r_ref[rows] = inv
            a_ref[rows] = (res[:, :DH] * inv).astype(BF)


def attend_chunk(q, k, v, loc, prior, chunk):
    first = pl.BlockSpec((BLOCK, DH), lambda h: (2 * chunk, h))
    second = pl.BlockSpec((BLOCK, DH), lambda h: (2 * chunk + 1, h))
    own = pl.BlockSpec((BLOCK, DH), lambda h: (0, h))
    return pl.pallas_call(
        attend_kernel,
        grid=(NH,),
        in_specs=[first, second] * 3
        + [
            pl.BlockSpec((2, 1, ROWS, DH), lambda h: (chunk, h, 0, 0)),
            pl.BlockSpec((1, ROWS, DH), lambda h: (h, 0, 0)),
        ],
        out_specs=[own] * 4,
        out_shape=[jax.ShapeDtypeStruct((BLOCK, NH * DH), BF)] * 2
        + [jax.ShapeDtypeStruct((BLOCK, NH * DH), F32)] * 2,
        compiler_params=PARAMS,
        name="attend",
    )(q, q, k, k, v, v, loc, prior)


def project_kernel(
    dims, place, xa, xb, ga, gb, wh, wx, wd, am, ao, bm, bo, keep_a, keep_b, to_x, to_d
):
    even = place[3] == 0
    a_h = jnp.where(even, am[...], ao[...])
    a_d = jnp.where(even, ao[...], am[...])
    b_h = jnp.where(even, bm[...], bo[...])
    b_x = jnp.where(even, bo[...], bm[...])
    own = wh[...]
    if dims == NT:
        ka, sa, kb, sb = wx[...], (b_h, b_x), wd[...], (a_h, a_d)
    else:
        ka, sa, kb, sb = a_h, (wd[...], a_d), b_h, (wx[...], b_x)
    keep_a[...] = dot(xa[...], own, dims) + dot(ga[...], ka, dims)
    to_d[...] = (dot(xa[...], sa[0], dims) + dot(ga[...], sa[1], dims)).astype(BF)
    keep_b[...] = dot(xb[...], own, dims) + dot(gb[...], kb, dims)
    to_x[...] = (dot(xb[...], sb[0], dims) + dot(gb[...], sb[1], dims)).astype(BF)


def project(dims, place, xa, xb, offset, ga, gb, weight, remote, steps=2):
    size = NH * DH
    rows = BLOCK // steps
    tile = pl.BlockSpec((rows, size), lambda i, s: (i, 0))
    whole = pl.BlockSpec((size, size), lambda i, s: (0, 0))

    def part(slot):
        return pl.BlockSpec((size, size), lambda i, s: (0, s[slot]))

    def at(block):
        return pl.BlockSpec((rows, size), lambda i, s: (block * steps + i, 0))

    return pl.pallas_call(
        functools.partial(project_kernel, dims),
        grid_spec=pltpu.PrefetchScalarGridSpec(
            num_scalar_prefetch=1,
            grid=(steps,),
            in_specs=[at(offset[0]), at(offset[1]), tile, tile, part(0), part(1), part(2)]
            + [whole] * 4,
            out_specs=[tile] * 4,
        ),
        out_shape=[jax.ShapeDtypeStruct((BLOCK, size), F32)] * 2
        + [jax.ShapeDtypeStruct((BLOCK, size), BF)] * 2,
        compiler_params=PARAMS,
        name="project",
    )(place, xa, xb, ga, gb, weight, weight, weight, *remote)


def numden_kernel(q0, q1, a0, a1, r0, r1, k0, k1, p0, p1, gn_ref, den_ref, sum_ref):
    head = pl.program_id(0)
    lane = lax.broadcasted_iota(jnp.int32, (BLOCK, DH), 1)

    @pl.when(head == 0)
    def _():
        den_ref[...] = jnp.zeros_like(den_ref)

    for block, (q_ref, a_ref, r_ref, k_ref, p_ref) in enumerate(
        ((q0, a0, r0, k0, p0), (q1, a1, r1, k1, p1))
    ):
        rows = slice(block * BLOCK, (block + 1) * BLOCK)
        fq = feature(q_ref[...].astype(F32)).astype(BF)
        grad = k_ref[...] + p_ref[...].astype(F32)
        inv = r_ref[...]
        num = (grad * inv).astype(BF)
        gn_ref[rows] = num
        den = -jnp.sum(grad * a_ref[...].astype(F32), axis=1, keepdims=True) * inv
        upper = den.astype(BF)
        rest = (den - upper.astype(F32)).astype(BF)
        den_ref[rows] = jnp.where(
            lane == 2 * head, upper, jnp.where(lane == 2 * head + 1, rest, den_ref[rows])
        )
        sum_ref[block, 0, :DH] = dot(num, fq, TN)
        z = jnp.sum(den * fq.astype(F32), axis=0, keepdims=True)
        sum_ref[block, 0, DH:] = jnp.broadcast_to(z, (ROWS - DH, DH))


def numden(q, a, r, keep, got, chunk):
    first = pl.BlockSpec((BLOCK, DH), lambda h: (2 * chunk, h))
    second = pl.BlockSpec((BLOCK, DH), lambda h: (2 * chunk + 1, h))
    own = pl.BlockSpec((BLOCK, DH), lambda h: (0, h))
    return pl.pallas_call(
        numden_kernel,
        grid=(NH,),
        in_specs=[first, second] + [own] * 8,
        out_specs=[
            pl.BlockSpec((2 * BLOCK, DH), lambda h: (0, h)),
            pl.BlockSpec((2 * BLOCK, DH), lambda h: (0, 0)),
            pl.BlockSpec((2, 1, ROWS, DH), lambda h: (0, h, 0, 0)),
        ],
        out_shape=[
            jax.ShapeDtypeStruct((2 * BLOCK, NH * DH), BF),
            jax.ShapeDtypeStruct((2 * BLOCK, DH), BF),
            jax.ShapeDtypeStruct((2, NH, ROWS, DH), F32),
        ],
        compiler_params=PARAMS,
        name="numden",
    )(q, q, *a, *r, *keep, *got)


def local_kernel(q_ref, k_ref, v_ref, n_ref, d_ref, loc_ref, prior_ref, *rest):
    gq_ref, gk_ref, gv_ref = rest[-3:]
    upper = lax.broadcasted_iota(jnp.int32, (HALF, HALF), 0) <= lax.broadcasted_iota(
        jnp.int32, (HALF, HALF), 1
    )
    lane = lax.broadcasted_iota(jnp.int32, (BLOCK, DH), 1)
    top, low = slice(0, HALF), slice(HALF, BLOCK)
    dens = d_ref[...]
    for head in range(NH):
        col = cols(head)
        queries = q_ref[:, col].astype(F32)
        raw = feature(queries)
        fq = raw.astype(BF)
        fk = feature(k_ref[:, col].astype(F32)).astype(BF)
        num = n_ref[:, col]
        pick = ((lane == 2 * head) | (lane == 2 * head + 1)).astype(F32).astype(BF)
        left = jnp.concatenate([v_ref[:, col], pick], axis=1)
        right = jnp.concatenate([num, dens], axis=1)

        def pair(a, b, s, t, mask):
            out = dot(a[s], b[t], NT)
            return (jnp.where(upper, out, 0.0) if mask else out).astype(BF)

        w00 = pair(fk, fq, top, top, True)
        w01 = pair(fk, fq, top, low, False)
        w11 = pair(fk, fq, low, low, True)
        g00 = pair(left, right, top, top, True)
        g01 = pair(left, right, top, low, False)
        g11 = pair(left, right, low, low, True)
        gv_ref[top, col] = dot(jnp.concatenate([w00, w01], axis=1), num, NN)
        gv_ref[low, col] = dot(w11, num[low], NN)
        gk_ref[top, col] = dot(jnp.concatenate([g00, g01], axis=1), fq, NN)
        gk_ref[low, col] = dot(g11, fq[low], NN)
        state = prior_ref[head] + loc_ref[0, head]
        past = dot(
            jnp.concatenate([num, num], axis=1),
            jnp.concatenate(halves(state[:DH]), axis=0),
            NN,
        )
        den = dens[:, 2 * head : 2 * head + 1].astype(F32) + dens[
            :, 2 * head + 1 : 2 * head + 2
        ].astype(F32)
        past = past + den * state[DH : DH + 1]
        tilt = jnp.minimum(raw, 1.0)
        gq_ref[top, col] = (tilt[top] * (past[top] + dot(g00, fk[top], TN))).astype(BF)
        gq_ref[low, col] = (
            tilt[low]
            * (past[low] + dot(jnp.concatenate([g01, g11], axis=0), fk, TN))
        ).astype(BF)


def local(q, k, v, num, den, loc, prior, chunk, earlier):
    wide = pl.BlockSpec((BLOCK, NH * DH), lambda b: (2 * chunk + b, 0))
    near = pl.BlockSpec((BLOCK, NH * DH), lambda b: (b, 0))
    full = (NB * BLOCK, NH * DH)
    extra = () if earlier is None else tuple(earlier)
    return pl.pallas_call(
        local_kernel,
        grid=(2,),
        in_specs=[
            wide,
            wide,
            wide,
            near,
            pl.BlockSpec((BLOCK, DH), lambda b: (b, 0)),
            pl.BlockSpec((1, NH, ROWS, DH), lambda b: (2 * chunk + b, 0, 0, 0)),
            pl.BlockSpec((NH, ROWS, DH), lambda b: (0, 0, 0)),
        ]
        + [pl.BlockSpec(memory_space=pl.ANY)] * len(extra),
        out_specs=[wide] * 3,
        out_shape=[
            jax.ShapeDtypeStruct(full, BF),
            jax.ShapeDtypeStruct(full, F32),
            jax.ShapeDtypeStruct(full, F32),
        ],
        input_output_aliases={7 + i: i for i in range(len(extra))},
        compiler_params=PARAMS,
        name="local",
    )(q, k, v, num, den, loc, prior, *extra)


def later_kernel(k_ref, v_ref, gk_in, gv_in, s0_ref, s1_ref, after_ref, gk_ref, gv_ref):
    state = after_ref[0]
    for block in reversed(range(NB)):
        rows = slice(block * BLOCK, (block + 1) * BLOCK)
        raw = feature(k_ref[rows].astype(F32))
        fk = raw.astype(BF)
        upper, rest = halves(state[:DH])
        val = v_ref[rows]
        gk = gk_in[rows] + dot(
            jnp.concatenate([val, val], axis=1), jnp.concatenate([upper, rest], axis=0), NN
        )
        gk = gk + state[DH : DH + 1]
        gk_ref[rows] = (jnp.minimum(raw, 1.0) * gk).astype(BF)
        gv = gv_in[rows] + dot(
            jnp.concatenate([fk, fk], axis=1), jnp.concatenate([upper, rest], axis=1), NT
        )
        gv_ref[rows] = gv.astype(BF)
        if block:
            state = state + (s0_ref, s1_ref)[block // 2][block % 2, 0]


def later(k, v, gk, gv, s0, s1, after):
    tall = pl.BlockSpec((NB * BLOCK, DH), lambda h: (0, h))
    sums = pl.BlockSpec((2, 1, ROWS, DH), lambda h: (0, h, 0, 0))
    return pl.pallas_call(
        later_kernel,
        grid=(NH,),
        in_specs=[tall] * 4 + [sums, sums, pl.BlockSpec((1, ROWS, DH), lambda h: (h, 0, 0))],
        out_specs=[tall] * 2,
        out_shape=[jax.ShapeDtypeStruct((NB * BLOCK, NH * DH), BF)] * 2,
        compiler_params=PARAMS,
        name="later",
    )(k, v, gk, gv, s0, s1, after)


A_PAIRS = [(h, h ^ 1) for h in range(4)]
B_PAIRS = [(h, 3 - h) for h in range(4)]


def ctx_pairs(change):
    out = []
    for y in range(4):
        for z in range(4):
            for c in range(2):
                y2, z2, c2 = change(y, z, c)
                out.append((y * 8 + z * 2 + c, y2 * 8 + z2 * 2 + c2))
    return out


def swap(x, change):
    return lax.ppermute(x, "ctx", ctx_pairs(change))


def sibling(x):
    return swap(x, lambda y, z, c: (y, z, 1 - c))


def entering(total, reverse):
    index = lax.axis_index("ctx")
    core, z, y = index % 2, (index // 2) % 4, index // 8
    second_core = (core == 0) if reverse else (core == 1)
    odd_z = (z % 2 == 0) if reverse else (z % 2 == 1)
    high_z = (z < 2) if reverse else (z >= 2)
    odd_y = (y % 2 == 0) if reverse else (y % 2 == 1)
    high_y = (y < 2) if reverse else (y >= 2)
    parts = total.reshape(2, 2, ROWS, DH)
    mine = lax.dynamic_index_in_dim(parts, core, 0, False)
    other = lax.dynamic_index_in_dim(parts, 1 - core, 0, False)
    got = sibling(other)
    chip = mine + got
    near = swap(chip, lambda y, z, c: (y ^ 1, z, c))
    pair = chip + near
    far = swap(pair, lambda y, z, c: (3 - y, z, c))
    column = jnp.where(odd_y, near, 0.0) + jnp.where(high_y, far, 0.0)
    both = swap(jnp.stack([column, chip]), lambda y, z, c: (y, z ^ 1, c))
    column2 = column + both[0]
    chip2 = chip + both[1]
    message = column2 + jnp.where(high_z, 0.0, chip2)
    more = swap(message, lambda y, z, c: (y, 3 - z, c))
    ahead = column2 + jnp.where(odd_z, both[1], 0.0) + more
    my = ahead + jnp.where(second_core, got, 0.0)
    its = ahead + jnp.where(second_core, 0.0, mine)
    back = sibling(its)
    lower = jnp.where(core == 0, my, back)
    upper = jnp.where(core == 0, back, my)
    return jnp.concatenate([lower, upper], axis=0)


def on_device(queries, key_input, value_input, out_weight, cotangent):
    head = lax.axis_index("head")
    core = lax.axis_index("ctx") % 2
    size = NH * DH
    place = jnp.stack([head, head ^ 1, 3 - head, core]).astype(jnp.int32)

    def to_x(x):
        return lax.ppermute(x, "head", A_PAIRS)

    def to_d(x):
        return lax.ppermute(x, "head", B_PAIRS)

    def rows(x, block):
        return lax.slice_in_dim(x, block * BLOCK, (block + 1) * BLOCK, axis=0)

    partner, across = head ^ 1, 3 - head
    a_cols = jnp.where(core == 0, partner, 3 - partner) * size
    b_cols = jnp.where(core == 0, across, across ^ 1) * size
    a_mine = to_x(lax.dynamic_slice_in_dim(out_weight, a_cols, size, 1))
    b_mine = to_d(lax.dynamic_slice_in_dim(out_weight, b_cols, size, 1))
    remote = (a_mine, sibling(a_mine), b_mine, sibling(b_mine))

    cots = [(to_x(rows(cotangent, 2 * c)), to_d(rows(cotangent, 2 * c + 1))) for c in range(2)]
    loc, total = totals(key_input, value_input)
    prior = entering(total, False)

    grads = []
    for c in range(2):
        keep_a, keep_b, send_x, send_d = project(
            NT, place, cotangent, cotangent, (2 * c, 2 * c + 1), *cots[c], out_weight, remote
        )
        grads.append(((keep_a, keep_b), (to_d(send_d), to_x(send_x))))

    heads = [attend_chunk(queries, key_input, value_input, loc, prior, c) for c in range(2)]
    gathered = [(to_x(heads[c][0]), to_d(heads[c][1])) for c in range(2)]

    nums = [numden(queries, heads[c][:2], heads[c][2:], *grads[c], c) for c in range(2)]
    sums0, sums1 = nums[0][2], nums[1][2]
    after = entering(jnp.sum(sums0, 0) + jnp.sum(sums1, 0), True)

    outs = []
    for c in range(2):
        keep_a, keep_b, send_x, send_d = project(
            NN, place, heads[c][0], heads[c][1], (0, 0), *gathered[c], out_weight, remote
        )
        outs.append((keep_a + to_d(send_d).astype(F32)).astype(BF))
        outs.append((keep_b + to_x(send_x).astype(F32)).astype(BF))
    layer_out = jnp.concatenate(outs, axis=0)

    state = None
    for c in range(2):
        state = local(
            queries, key_input, value_input, nums[c][0], nums[c][1], loc, prior, c, state
        )
    grad_query, near_k, near_v = state
    grad_key, grad_value = later(
        key_input, value_input, near_k, near_v, sums0, sums1, after
    )
    return (layer_out, grad_query, grad_key, grad_value)


def solution(mesh):
    in_specs = (
        P("ctx", "head"),
        P("ctx", "head"),
        P("ctx", "head"),
        P("head", None),
        P("ctx", "head"),
    )
    out_specs = (P("ctx", "head"), P("ctx", "head"), P("ctx", "head"), P("ctx", "head"))
    return jax.shard_map(
        on_device, mesh=mesh, in_specs=in_specs, out_specs=out_specs, check_vma=False
    )
```

time: 412 us -> 168 us (0.41)
  waiting for transfers between devices: 104 us -> 18.4 us
  Pallas kernels: 0 us -> 82.4 us
  matrix products: 81.7 us -> 0 us
  blocking collectives: 80.9 us -> 0 us
  local copies, waits for them, and re-layouts: 67.9 us -> 7.64 us
  other arithmetic: 59.9 us -> 7.79 us
  starting transfers between devices: 0.16 us -> 50.2 us
  between operations: 14.1 us -> 0.99 us
    pallas_call x0 -> x12, Pallas kernels: none -> 82.4 us  [the longest x4 26.7 us: project(): pl.pallas_call(functools.partial(project_kernel, dims), grid_spec=pltpu.P...]
    dot_general x20 -> x0, matrix products: 81.7 us -> none  [the longest x1 9.63 us: on_device(): jnp.dot(attn_rows, out_weight, preferred_element_type=jnp.float32)]
    all_gather x2 -> x0, blocking collectives: 80.9 us -> none  [entering(): gathered = jax.tree.map(lambda a: lax.all_gather(a, axis), part)]
    all_gather x3 -> x0, waiting for transfers between devices: 51.7 us -> none  [the longest x2 36.6 us: entering(): gathered = jax.tree.map(lambda a: lax.all_gather(a, axis), part)]
    reduce_scatter x1 -> x0, waiting for transfers between devices: 51.7 us -> none  [on_device(): lax.psum_scatter(partial_out, 'head', scatter_dimension=1, tiled=True)]
    ppermute x0 -> x32, starting transfers between devices: none -> 50.2 us  [the longest x14 29.9 us: swap(): return lax.ppermute(x, 'ctx', ctx_pairs(change))]
    reshape x7 -> x0, local copies, waits for them, and re-layouts: 31 us -> none  [the longest x2 10.6 us: on_device(): grad_attn = jnp.einsum('tc,wc->tw', lax.all_gather(cotangent, 'head', axi...]
    add x65 -> x11, other arithmetic: 32.2 us -> 1.23 us  [the longest x2 0.94 us: entering(): chip = mine + got]
  transfers between devices with their start and end apart: 4 -> 32, of which waited for: 3 -> 9; matrix products, arithmetic and copies ran while one was open for 44% -> 5% of each run, Pallas kernels for 0% -> 41%
where the time goes in v1:
time: 168 us; the launch traced here: 167 us
  Pallas kernels  82.4 us (49%)
  starting transfers between devices  50.2 us (30%)
  waiting for transfers between devices  18.4 us (11%)
  other arithmetic  7.79 us (5%)
  local copies, waits for them, and re-layouts  7.64 us (5%)
    ppermute x14, starting transfers between devices, swap(): return lax.ppermute(x, 'ctx', ctx_pairs(change))  29.9 us
    pallas_call x4, Pallas kernels, project(): pl.pallas_call(functools.partial(project_kernel, dims), grid_spec=pltpu.P...  26.7 us
    pallas_call x2, Pallas kernels, local(): pl.pallas_call(local_kernel, grid=(2,), in_specs=[wide, wide, wide, near,...  17.5 us
    ppermute x9, starting transfers between devices, to_d(): return lax.ppermute(x, 'head', B_PAIRS)  14.3 us
    pallas_call x2, Pallas kernels, attend_chunk(): pl.pallas_call(attend_kernel, grid=(NH,), in_specs=[first, second] * 3 +...  13.2 us
    pallas_call x2, Pallas kernels, numden(): pl.pallas_call(numden_kernel, grid=(NH,), in_specs=[first, second] + [own...  11.4 us
    ppermute x14, waiting for transfers between devices, swap(): return lax.ppermute(x, 'ctx', ctx_pairs(change))  10 us
    pallas_call x1, Pallas kernels, later(): pl.pallas_call(later_kernel, grid=(NH,), in_specs=[tall] * 4 + [sums, sum...  8.38 us
  transfers between devices with their start and end apart: 32, of which 9 were waited for; matrix products, arithmetic and copies ran while one was open for 5% of the time, Pallas kernels for 41%

profile of v1, /device:TPU:1, one launch (start us, length us, event | category | flops | bytes accessed | tf_op | source)
XLA Modules:
  0.0 167.4 jit_solution(9255728458995616227)
XLA Ops:
  0.7 5.2 %totals.1 = (f32[4,4,136,128]{3,2,1,0:T(8,128)}, f32[4,136,128]{2,1,0:T(8,128)}) custom-call(bf16[2048,512]{1,0:T(8,128)(2,1)} %k_ref.7, bf16[2048,512]{1,0:T(8,128)(2,1)} %v_ref.7), custom_call_target="tpu_custom_call" | custom-call | tf_op jit(solution)/shard_map/totals/pallas_call | solution.py:64
  5.9 0.9 dynamic-slice_bitcast_fusion.1
  6.8 1.5 collective-permute-start
  8.3 1.0 collective-permute-done
  9.3 0.9 bitcast_add_fusion.1
  10.2 1.5 collective-permute-start.1
  11.7 0.9 constant_dynamic-slice_fusion
  12.6 1.2 collective-permute-start.8
  13.8 1.8 %collective-permute-start.10 = (bf16[512,512]{1,0:T(8,128)(2,1)S(1)}, bf16[512,512]{1,0:T(8,128)(2,1)S(1)}, u32[]{:S(2)}, u32[]{:S(2)}) collective-permute-start(bf16[512,512]{1,0:T(8,128)(2,1)S(1)} %get-tuple-element.92), channel_id=1, source_target_pairs={{0,3},{1,2},{2,1},{3,0},{4,7},{5,6},{6,5},{7,4},{8,11},{9,10},{10,... | collective-permute-start | bytes 1572872 | tf_op jit(solution)/shard_map/ppermute | solution.py:410
  15.6 2.5 %collective-permute-start.2 = (f32[2,136,128]{2,1,0:T(8,128)S(1)}, f32[2,136,128]{2,1,0:T(8,128)S(1)}, u32[]{:S(2)}, u32[]{:S(2)}) collective-permute-start(f32[2,136,128]{2,1,0:T(8,128)S(1)} %add.120), channel_id=1, source_target_pairs={{0,96},{4,100},{8,104},{12,108},{16,112},{20,116},{24,120},{28,124... | collective-permute-start | bytes 417800 | tf_op jit(solution)/shard_map/ppermute | solution.py:362
  18.1 1.4 fusion.4
  19.4 1.2 collective-permute-start.18
  20.7 0.5 collective-permute-done.2
  21.2 1.7 %collective-permute-start.3 = (f32[2,2,136,128]{3,2,1,0:T(8,128)S(1)}, f32[2,2,136,128]{3,2,1,0:T(8,128)S(1)}, u32[]{:S(2)}, u32[]{:S(2)}) collective-permute-start(f32[2,2,136,128]{3,2,1,0:T(8,128)S(1)} %pad_maximum_fusion.1), channel_id=1, source_target_pairs={{0,8},{4,12},{8,0},{12,4},{16,24},{20,28},{24,16},{28,20},{32,40},... | collective-permute-start | bytes 835592 | tf_op jit(solution)/shard_map/ppermute | solution.py:362
  22.9 2.2 %collective-permute-start.19 = (bf16[512,512]{1,0:T(8,128)(2,1)}, bf16[512,512]{1,0:T(8,128)(2,1)}, u32[]{:S(2)}, u32[]{:S(2)}) collective-permute-start(bf16[512,512]{1,0:T(8,128)(2,1)} %get-tuple-element.90), channel_id=1, source_target_pairs={{0,3},{1,2},{2,1},{3,0},{4,7},{5,6},{6,5},{7,4},{8,11},{9,10},{10,... | collective-permute-start | bytes 1572872 | tf_op jit(solution)/shard_map/ppermute | solution.py:410
  25.1 0.6 collective-permute-done.8.am
  25.6 2.6 %collective-permute-start.9 = (bf16[512,512]{1,0:T(8,128)(2,1)S(1)}, bf16[512,512]{1,0:T(8,128)(2,1)S(1)}, u32[]{:S(2)}, u32[]{:S(2)}) collective-permute-start(bf16[512,512]{1,0:T(8,128)(2,1)S(1)} %collective-permute-done.8.am), channel_id=1, source_target_pairs={{0,4},{4,0},{8,12},{12,8},{16,20},{20,16},{24,28},{28,24},{32,36},... | collective-permute-start | bytes 1572872 | tf_op jit(solution)/shard_map/ppermute | solution.py:362
  28.2 2.5 %collective-permute-start.11 = (bf16[512,512]{1,0:T(8,128)(2,1)S(1)}, bf16[512,512]{1,0:T(8,128)(2,1)S(1)}, u32[]{:S(2)}, u32[]{:S(2)}) collective-permute-start(bf16[512,512]{1,0:T(8,128)(2,1)S(1)} %collective-permute-done.10.bm), channel_id=1, source_target_pairs={{0,4},{4,0},{8,12},{12,8},{16,20},{20,16},{24,28},{28,24},{32,36},... | collective-permute-start | bytes 1572872 | tf_op jit(solution)/shard_map/ppermute | solution.py:362
  30.8 6.2 %collective-permute-done.18.ga = bf16[512,512]{1,0:T(8,128)(2,1)} collective-permute-done((bf16[512,512]{1,0:T(8,128)(2,1)}, bf16[512,512]{1,0:T(8,128)(2,1)}, u32[]{:S(2)}, u32[]{:S(2)}) %collective-permute-start.18) | collective-permute-done | bytes 524320 | tf_op jit(solution)/shard_map/ppermute | solution.py:407
  37.0 1.2 collective-permute-start.22
  38.2 1.8 %collective-permute-start.23 = (bf16[512,512]{1,0:T(8,128)(2,1)}, bf16[512,512]{1,0:T(8,128)(2,1)}, u32[]{:S(2)}, u32[]{:S(2)}) collective-permute-start(bf16[512,512]{1,0:T(8,128)(2,1)} %get-tuple-element.88), channel_id=1, source_target_pairs={{0,3},{1,2},{2,1},{3,0},{4,7},{5,6},{6,5},{7,4},{8,11},{9,10},{10,... | collective-permute-start | bytes 1572872 | tf_op jit(solution)/shard_map/ppermute | solution.py:410
  40.1 3.8 %collective-permute-start.4 = (f32[2,136,128]{2,1,0:T(8,128)S(1)}, f32[2,136,128]{2,1,0:T(8,128)S(1)}, u32[]{:S(2)}, u32[]{:S(2)}) collective-permute-start(f32[2,136,128]{2,1,0:T(8,128)S(1)} %select_add_fusion.4), channel_id=1, source_target_pairs={{0,24},{4,28},{8,16},{12,20},{16,8},{20,12},{24,0},{28,4},{32,56},... | collective-permute-start | bytes 417800 | tf_op jit(solution)/shard_map/ppermute | solution.py:362
  43.9 0.7 pad_add_fusion.place
  44.6 0.8 copy-done.4
  45.3 0.8 copy-done.5
  46.2 6.8 %project.6 = (f32[512,512]{1,0:T(8,128)}, f32[512,512]{1,0:T(8,128)}, bf16[512,512]{1,0:T(8,128)(2,1)}, bf16[512,512]{1,0:T(8,128)(2,1)}) custom-call(s32[4]{0:T(128)} %pad_add_fusion.place, bf16[2048,512]{1,0:T(8,128)(2,1)} %xb.3, bf16[2048,512]{1,0:T(8,128)(2,1)} %xb.3, bf16[512,512]{1,0:T(8,128)(2,1)} %collective-permute-done.18.ga, ...), custom_call_target="tpu_custom_call" | custom-call | tf_op jit(solution)/shard_map/project/pallas_call | solution.py:164
  52.9 0.9 collective-permute-start.20
  53.9 6.8 %project.7 = (f32[512,512]{1,0:T(8,128)}, f32[512,512]{1,0:T(8,128)}, bf16[512,512]{1,0:T(8,128)(2,1)}, bf16[512,512]{1,0:T(8,128)(2,1)}) custom-call(s32[4]{0:T(128)} %pad_add_fusion.place, bf16[2048,512]{1,0:T(8,128)(2,1)} %xb.3, bf16[2048,512]{1,0:T(8,128)(2,1)} %xb.3, bf16[512,512]{1,0:T(8,128)(2,1)} %collective-permute-done.22.ga, ...), custom_call_target="tpu_custom_call" | custom-call | tf_op jit(solution)/shard_map/project/pallas_call | solution.py:164
  60.7 1.9 %collective-permute-start.24 = (bf16[512,512]{1,0:T(8,128)(2,1)}, bf16[512,512]{1,0:T(8,128)(2,1)S(1)}, u32[]{:S(2)}, u32[]{:S(2)}) collective-permute-start(bf16[512,512]{1,0:T(8,128)(2,1)} %get-tuple-element.70), channel_id=1, source_target_pairs={{0,3},{1,2},{2,1},{3,0},{4,7},{5,6},{6,5},{7,4},{8,11},{9,10},{10,... | collective-permute-start | bytes 1572872 | tf_op jit(solution)/shard_map/ppermute | solution.py:410
  62.6 0.7 collective-permute-start.25
  63.3 3.5 %collective-permute-start.5 = (f32[2,136,128]{2,1,0:T(8,128)S(1)}, f32[2,136,128]{2,1,0:T(8,128)S(1)}, u32[]{:S(2)}, u32[]{:S(2)}) collective-permute-start(f32[2,136,128]{2,1,0:T(8,128)S(1)} %get-tuple-element.86), channel_id=1, source_target_pairs={{0,4},{4,0},{8,12},{12,8},{16,20},{20,16},{24,28},{28,24},{32,36},... | collective-permute-start | bytes 417800 | tf_op jit(solution)/shard_map/ppermute | solution.py:362
  66.9 1.0 collective-permute-done.5
  67.9 0.7 pad_maximum_fusion.2.prior_ref
  68.6 6.6 %attend.3 = (bf16[512,512]{1,0:T(8,128)(2,1)}, bf16[512,512]{1,0:T(8,128)(2,1)}, f32[512,512]{1,0:T(8,128)}, f32[512,512]{1,0:T(8,128)}) custom-call(bf16[2048,512]{1,0:T(8,128)(2,1)} %q_ref.3, bf16[2048,512]{1,0:T(8,128)(2,1)} %q_ref.3, bf16[2048,512]{1,0:T(8,128)(2,1)} %k_ref.7, bf16[2048,512]{1,0:T(8,128)(2,1)} %k_ref.7, bf16[2048,512]{1,0:T(8,128)(2,1)} %v_ref.7, ...), custom_call_target="tpu_custom_call" | custom-call | tf_op jit(solution)/shard_map/attend/pallas_call | solution.py:117
  75.2 6.7 %attend.2 = (bf16[512,512]{1,0:T(8,128)(2,1)}, bf16[512,512]{1,0:T(8,128)(2,1)}, f32[512,512]{1,0:T(8,128)}, f32[512,512]{1,0:T(8,128)}) custom-call(bf16[2048,512]{1,0:T(8,128)(2,1)} %q_ref.3, bf16[2048,512]{1,0:T(8,128)(2,1)} %q_ref.3, bf16[2048,512]{1,0:T(8,128)(2,1)} %k_ref.7, bf16[2048,512]{1,0:T(8,128)(2,1)} %k_ref.7, bf16[2048,512]{1,0:T(8,128)(2,1)} %v_ref.7, ...), custom_call_target="tpu_custom_call" | custom-call | tf_op jit(solution)/shard_map/attend/pallas_call | solution.py:117
  81.9 0.6 collective-permute-start.14
  82.5 1.1 collective-permute-start.15
  83.6 0.8 copy-done.18
  84.4 5.7 %numden.3 = (bf16[1024,512]{1,0:T(8,128)(2,1)}, bf16[1024,128]{1,0:T(8,128)(2,1)}, f32[2,4,136,128]{3,2,1,0:T(8,128)}) custom-call(bf16[2048,512]{1,0:T(8,128)(2,1)} %q_ref.3, bf16[2048,512]{1,0:T(8,128)(2,1)} %q_ref.3, bf16[512,512]{1,0:T(8,128)(2,1)} %get-tuple-element.46.xa.a0, bf16[512,512]{1,0:T(8,128)(2,1)} %get-tuple-element.47.xb.a1, ...), custom_call_target="tpu_custom_call" | custom-call | tf_op jit(solution)/shard_map/numden/pallas_call | solution.py:212
  90.1 1.1 reduce_sum.18
  91.2 0.8 copy-done.16
  92.2 5.7 %numden.2 = (bf16[1024,512]{1,0:T(8,128)(2,1)}, bf16[1024,128]{1,0:T(8,128)(2,1)}, f32[2,4,136,128]{3,2,1,0:T(8,128)}) custom-call(bf16[2048,512]{1,0:T(8,128)(2,1)} %q_ref.3, bf16[2048,512]{1,0:T(8,128)(2,1)} %q_ref.3, bf16[512,512]{1,0:T(8,128)(2,1)} %get-tuple-element.52.xa.a0, bf16[512,512]{1,0:T(8,128)(2,1)} %get-tuple-element.53.xb.a1, ...), custom_call_target="tpu_custom_call" | custom-call | tf_op jit(solution)/shard_map/numden/pallas_call | solution.py:212
  97.9 1.1 reduce_sum.19
  99.1 1.0 collective-permute-start.26
  100.1 0.4 collective-permute-start.6
  100.5 1.8 %collective-permute-start.7 = (bf16[512,512]{1,0:T(8,128)(2,1)S(1)}, bf16[512,512]{1,0:T(8,128)(2,1)}, u32[]{:S(2)}, u32[]{:S(2)}) collective-permute-start(bf16[512,512]{1,0:T(8,128)(2,1)S(1)} %copy-done.7), channel_id=1, source_target_pairs={{0,3},{1,2},{2,1},{3,0},{4,7},{5,6},{6,5},{7,4},{8,11},{9,10},{10,... | collective-permute-start | bytes 1572872 | tf_op jit(solution)/shard_map/ppermute | solution.py:410
  102.6 6.5 %project.5 = (f32[512,512]{1,0:T(8,128)}, f32[512,512]{1,0:T(8,128)}, bf16[512,512]{1,0:T(8,128)(2,1)}, bf16[512,512]{1,0:T(8,128)(2,1)}) custom-call(s32[4]{0:T(128)} %pad_add_fusion.place, bf16[512,512]{1,0:T(8,128)(2,1)} %get-tuple-element.52.xa.a0, bf16[512,512]{1,0:T(8,128)(2,1)} %get-tuple-element.53.xb.a1, ...), custom_call_target="tpu_custom_call" | custom-call | tf_op jit(solution)/shard_map/project/pallas_call | solution.py:164
  109.1 0.6 collective-permute-start.17
  109.7 2.8 %collective-permute-start.28 = (f32[2,136,128]{2,1,0:T(8,128)S(1)}, f32[2,136,128]{2,1,0:T(8,128)S(1)}, u32[]{:S(2)}, u32[]{:S(2)}) collective-permute-start(f32[2,136,128]{2,1,0:T(8,128)S(1)} %add.140), channel_id=1, source_target_pairs={{0,96},{4,100},{8,104},{12,108},{16,112},{20,116},{24,120},{28,124... | collective-permute-start | bytes 417800 | tf_op jit(solution)/shard_map/ppermute | solution.py:362
  112.6 0.9 collective-permute-start.16
  113.4 0.3 collective-permute-done.6.ga
  113.7 1.3 collective-permute-done.7.gb
  115.0 6.6 %project.4 = (f32[512,512]{1,0:T(8,128)}, f32[512,512]{1,0:T(8,128)}, bf16[512,512]{1,0:T(8,128)(2,1)}, bf16[512,512]{1,0:T(8,128)(2,1)}) custom-call(s32[4]{0:T(128)} %pad_add_fusion.place, bf16[512,512]{1,0:T(8,128)(2,1)} %get-tuple-element.46.xa.a0, bf16[512,512]{1,0:T(8,128)(2,1)} %get-tuple-element.47.xb.a1, bf16[512,512]{1,0:T(8,128)(2,1)} %copy-done.19, ...), custom_call_target="tpu_custom_call" | custom-call | tf_op jit(solution)/shard_map/project/pallas_call | solution.py:164
  121.6 1.9 %collective-permute-start.12 = (bf16[512,512]{1,0:T(8,128)(2,1)}, bf16[512,512]{1,0:T(8,128)(2,1)S(1)}, u32[]{:S(2)}, u32[]{:S(2)}) collective-permute-start(bf16[512,512]{1,0:T(8,128)(2,1)} %get-tuple-element.49), channel_id=1, source_target_pairs={{0,3},{1,2},{2,1},{3,0},{4,7},{5,6},{6,5},{7,4},{8,11},{9,10},{10,... | collective-permute-start | bytes 1572872 | tf_op jit(solution)/shard_map/ppermute | solution.py:410
  123.5 8.7 %local.2 = (bf16[2048,512]{1,0:T(8,128)(2,1)}, f32[2048,512]{1,0:T(8,128)}, f32[2048,512]{1,0:T(8,128)}) custom-call(bf16[2048,512]{1,0:T(8,128)(2,1)} %q_ref.3, bf16[2048,512]{1,0:T(8,128)(2,1)} %k_ref.7, bf16[2048,512]{1,0:T(8,128)(2,1)} %v_ref.7, bf16[1024,512]{1,0:T(8,128)(2,1)} %get-tuple-element.72.n_ref, bf16[1024,128]{1,0:T(8,128)(2,1)} %get-tuple-element.73.d_ref, ...), custom_call_target="tpu_custom_call" | custom-call | tf_op jit(solution)/shard_map/local/pallas_call | solution.py:287
  132.2 8.8 %local.3 = (bf16[2048,512]{1,0:T(8,128)(2,1)}, f32[2048,512]{1,0:T(8,128)}, f32[2048,512]{1,0:T(8,128)}) custom-call(bf16[2048,512]{1,0:T(8,128)(2,1)} %q_ref.3, bf16[2048,512]{1,0:T(8,128)(2,1)} %k_ref.7, bf16[2048,512]{1,0:T(8,128)(2,1)} %v_ref.7, ...), custom_call_target="tpu_custom_call", output_to_operand_aliasing={{0}: (7, {}), {1}: (8, {}), {2}: (9, {})} | custom-call | tf_op jit(solution)/shard_map/local/pallas_call | solution.py:287
  141.4 0.8 copy-done.10
  142.8 4.7 %collective-permute-done.29 = f32[2,2,136,128]{3,2,1,0:T(8,128)S(1)} collective-permute-done((f32[2,2,136,128]{3,2,1,0:T(8,128)S(1)}, f32[2,2,136,128]{3,2,1,0:T(8,128)S(1)}, u32[]{:S(2)}, u32[]{:S(2)}) %collective-permute-start.29) | collective-permute-done | bytes 278560 | tf_op jit(solution)/shard_map/ppermute | solution.py:362
  147.6 2.2 %collective-permute-start.30 = (f32[2,136,128]{2,1,0:T(8,128)S(1)}, f32[2,136,128]{2,1,0:T(8,128)S(1)}, u32[]{:S(2)}, u32[]{:S(2)}) collective-permute-start(f32[2,136,128]{2,1,0:T(8,128)S(1)} %select_add_fusion.1), channel_id=1, source_target_pairs={{0,24},{4,28},{8,16},{12,20},{16,8},{20,12},{24,0},{28,4},{32,56},... | collective-permute-start | bytes 417800 | tf_op jit(solution)/shard_map/ppermute | solution.py:362
  149.9 2.8 %collective-permute-done.30 = f32[2,136,128]{2,1,0:T(8,128)S(1)} collective-permute-done((f32[2,136,128]{2,1,0:T(8,128)S(1)}, f32[2,136,128]{2,1,0:T(8,128)S(1)}, u32[]{:S(2)}, u32[]{:S(2)}) %collective-permute-start.30) | collective-permute-done | bytes 139296 | tf_op jit(solution)/shard_map/ppermute | solution.py:362
  152.8 4.0 %collective-permute-start.31 = (f32[2,136,128]{2,1,0:T(8,128)S(1)}, f32[2,136,128]{2,1,0:T(8,128)S(1)}, u32[]{:S(2)}, u32[]{:S(2)}) collective-permute-start(f32[2,136,128]{2,1,0:T(8,128)S(1)} %get-tuple-element.84), channel_id=1, source_target_pairs={{0,4},{4,0},{8,12},{12,8},{16,20},{20,16},{24,28},{28,24},{32,36},... | collective-permute-start | bytes 417800 | tf_op jit(solution)/shard_map/ppermute | solution.py:362
  156.8 1.5 pad_maximum_fusion
  158.3 0.7 pad_maximum_fusion.4.after_ref
  159.0 8.4 %later.1 = (bf16[2048,512]{1,0:T(8,128)(2,1)}, bf16[2048,512]{1,0:T(8,128)(2,1)}) custom-call(bf16[2048,512]{1,0:T(8,128)(2,1)} %k_ref.7, bf16[2048,512]{1,0:T(8,128)(2,1)} %v_ref.7, f32[2048,512]{1,0:T(8,128)} %get-tuple-element.78.gk_in, f32[2048,512]{1,0:T(8,128)} %get-tuple-element.79.gv_in, f32[2,4,136,128]{3,2,1,0:T(8,128)} %get-tuple-element.80.s0_ref, ...), custom_call_target="tpu_custom_call" | custom-call | tf_op jit(solution)/shard_map/later/pallas_call | solution.py:336
  (81 shorter events, 1.9 us)
Async XLA Ops:
  0.6 11.0 %copy-start = (bf16[512,2048]{1,0:T(8,128)(2,1)S(1)}, bf16[512,2048]{1,0:T(8,128)(2,1)}, u32[]{:S(2)}) copy-start(bf16[512,2048]{1,0:T(8,128)(2,1)} %wd.7) | copy-start | bytes 6291460
  6.8 2.5 %collective-permute-start = (f32[2,136,128]{2,1,0:T(8,128)S(1)}, f32[2,136,128]{2,1,0:T(8,128)S(1)}, u32[]{:S(2)}, u32[]{:S(2)}) collective-permute-start(f32[2,136,128]{2,1,0:T(8,128)S(1)} %dynamic-slice_bitcast_fusion.1), channel_id=1, source_target_pairs={{0,4},{4,0},{8,12},{12,8},{16,20},{20,16},{24,28},{28,24},{32,36},... | collective-permute-start | bytes 417800 | tf_op jit(solution)/shard_map/ppermute | solution.py:362
  10.2 5.4 %collective-permute-start.1 = (f32[2,136,128]{2,1,0:T(8,128)S(1)}, f32[2,136,128]{2,1,0:T(8,128)S(1)}, u32[]{:S(2)}, u32[]{:S(2)}) collective-permute-start(f32[2,136,128]{2,1,0:T(8,128)S(1)} %bitcast_add_fusion.1), channel_id=1, source_target_pairs={{0,32},{4,36},{8,40},{12,44},{16,48},{20,52},{24,56},{28,60},{32,0... | collective-permute-start | bytes 417800 | tf_op jit(solution)/shard_map/ppermute | solution.py:362
  11.7 6.4 %copy-start.1 = (bf16[2048,512]{1,0:T(8,128)(2,1)S(1)}, bf16[2048,512]{1,0:T(8,128)(2,1)}, u32[]{:S(2)}) copy-start(bf16[2048,512]{1,0:T(8,128)(2,1)} %xb.3) | copy-start | bytes 6291460
  12.6 13.1 %collective-permute-start.8 = (bf16[512,512]{1,0:T(8,128)(2,1)}, bf16[512,512]{1,0:T(8,128)(2,1)S(1)}, u32[]{:S(2)}, u32[]{:S(2)}) collective-permute-start(bf16[512,512]{1,0:T(8,128)(2,1)} %get-tuple-element.93), channel_id=1, source_target_pairs={{0,1},{1,0},{2,3},{3,2},{4,5},{5,4},{6,7},{7,6},{8,9},{9,8},{10,11... | collective-permute-start | bytes 1572872 | tf_op jit(solution)/shard_map/ppermute | solution.py:407
  13.8 14.4 %collective-permute-start.10 = (bf16[512,512]{1,0:T(8,128)(2,1)S(1)}, bf16[512,512]{1,0:T(8,128)(2,1)S(1)}, u32[]{:S(2)}, u32[]{:S(2)}) collective-permute-start(bf16[512,512]{1,0:T(8,128)(2,1)S(1)} %get-tuple-element.92), channel_id=1, source_target_pairs={{0,3},{1,2},{2,1},{3,0},{4,7},{5,6},{6,5},{7,4},{8,11},{9,10},{10,... | collective-permute-start | bytes 1572872 | tf_op jit(solution)/shard_map/ppermute | solution.py:410
  15.6 5.5 %collective-permute-start.2 = (f32[2,136,128]{2,1,0:T(8,128)S(1)}, f32[2,136,128]{2,1,0:T(8,128)S(1)}, u32[]{:S(2)}, u32[]{:S(2)}) collective-permute-start(f32[2,136,128]{2,1,0:T(8,128)S(1)} %add.120), channel_id=1, source_target_pairs={{0,96},{4,100},{8,104},{12,108},{16,112},{20,116},{24,120},{28,124... | collective-permute-start | bytes 417800 | tf_op jit(solution)/shard_map/ppermute | solution.py:362
  19.4 17.5 %collective-permute-start.18 = (bf16[512,512]{1,0:T(8,128)(2,1)}, bf16[512,512]{1,0:T(8,128)(2,1)}, u32[]{:S(2)}, u32[]{:S(2)}) collective-permute-start(bf16[512,512]{1,0:T(8,128)(2,1)} %get-tuple-element.91), channel_id=1, source_target_pairs={{0,1},{1,0},{2,3},{3,2},{4,5},{5,4},{6,7},{7,6},{8,9},{9,8},{10,11... | collective-permute-start | bytes 1572872 | tf_op jit(solution)/shard_map/ppermute | solution.py:407
  21.2 17.0 %collective-permute-start.3 = (f32[2,2,136,128]{3,2,1,0:T(8,128)S(1)}, f32[2,2,136,128]{3,2,1,0:T(8,128)S(1)}, u32[]{:S(2)}, u32[]{:S(2)}) collective-permute-start(f32[2,2,136,128]{3,2,1,0:T(8,128)S(1)} %pad_maximum_fusion.1), channel_id=1, source_target_pairs={{0,8},{4,12},{8,0},{12,4},{16,24},{20,28},{24,16},{28,20},{32,40},... | collective-permute-start | bytes 835592 | tf_op jit(solution)/shard_map/ppermute | solution.py:362
  22.9 17.2 %collective-permute-start.19 = (bf16[512,512]{1,0:T(8,128)(2,1)}, bf16[512,512]{1,0:T(8,128)(2,1)}, u32[]{:S(2)}, u32[]{:S(2)}) collective-permute-start(bf16[512,512]{1,0:T(8,128)(2,1)} %get-tuple-element.90), channel_id=1, source_target_pairs={{0,3},{1,2},{2,1},{3,0},{4,7},{5,6},{6,5},{7,4},{8,11},{9,10},{10,... | collective-permute-start | bytes 1572872 | tf_op jit(solution)/shard_map/ppermute | solution.py:410
  25.6 18.9 %copy-start.2 = (bf16[512,512]{1,0:T(8,128)(2,1)}, bf16[512,512]{1,0:T(8,128)(2,1)S(1)}, u32[]{:S(2)}) copy-start(bf16[512,512]{1,0:T(8,128)(2,1)S(1)} %collective-permute-done.8.am) | copy-start | bytes 1572868
  25.6 18.9 %collective-permute-start.9 = (bf16[512,512]{1,0:T(8,128)(2,1)S(1)}, bf16[512,512]{1,0:T(8,128)(2,1)S(1)}, u32[]{:S(2)}, u32[]{:S(2)}) collective-permute-start(bf16[512,512]{1,0:T(8,128)(2,1)S(1)} %collective-permute-done.8.am), channel_id=1, source_target_pairs={{0,4},{4,0},{8,12},{12,8},{16,20},{20,16},{24,28},{28,24},{32,36},... | collective-permute-start | bytes 1572872 | tf_op jit(solution)/shard_map/ppermute | solution.py:362
  28.2 16.3 %copy-start.3 = (bf16[512,512]{1,0:T(8,128)(2,1)}, bf16[512,512]{1,0:T(8,128)(2,1)S(1)}, u32[]{:S(2)}) copy-start(bf16[512,512]{1,0:T(8,128)(2,1)S(1)} %collective-permute-done.10.bm) | copy-start | bytes 1572868
  28.2 16.3 %collective-permute-start.11 = (bf16[512,512]{1,0:T(8,128)(2,1)S(1)}, bf16[512,512]{1,0:T(8,128)(2,1)S(1)}, u32[]{:S(2)}, u32[]{:S(2)}) collective-permute-start(bf16[512,512]{1,0:T(8,128)(2,1)S(1)} %collective-permute-done.10.bm), channel_id=1, source_target_pairs={{0,4},{4,0},{8,12},{12,8},{16,20},{20,16},{24,28},{28,24},{32,36},... | collective-permute-start | bytes 1572872 | tf_op jit(solution)/shard_map/ppermute | solution.py:362
  37.0 16.9 %collective-permute-start.22 = (bf16[512,512]{1,0:T(8,128)(2,1)}, bf16[512,512]{1,0:T(8,128)(2,1)}, u32[]{:S(2)}, u32[]{:S(2)}) collective-permute-start(bf16[512,512]{1,0:T(8,128)(2,1)} %get-tuple-element.89), channel_id=1, source_target_pairs={{0,1},{1,0},{2,3},{3,2},{4,5},{5,4},{6,7},{7,6},{8,9},{9,8},{10,11... | collective-permute-start | bytes 1572872 | tf_op jit(solution)/shard_map/ppermute | solution.py:407
  38.2 15.7 %collective-permute-start.23 = (bf16[512,512]{1,0:T(8,128)(2,1)}, bf16[512,512]{1,0:T(8,128)(2,1)}, u32[]{:S(2)}, u32[]{:S(2)}) collective-permute-start(bf16[512,512]{1,0:T(8,128)(2,1)} %get-tuple-element.88), channel_id=1, source_target_pairs={{0,3},{1,2},{2,1},{3,0},{4,7},{5,6},{6,5},{7,4},{8,11},{9,10},{10,... | collective-permute-start | bytes 1572872 | tf_op jit(solution)/shard_map/ppermute | solution.py:410
  40.1 23.2 %collective-permute-start.4 = (f32[2,136,128]{2,1,0:T(8,128)S(1)}, f32[2,136,128]{2,1,0:T(8,128)S(1)}, u32[]{:S(2)}, u32[]{:S(2)}) collective-permute-start(f32[2,136,128]{2,1,0:T(8,128)S(1)} %select_add_fusion.4), channel_id=1, source_target_pairs={{0,24},{4,28},{8,16},{12,20},{16,8},{20,12},{24,0},{28,4},{32,56},... | collective-permute-start | bytes 417800 | tf_op jit(solution)/shard_map/ppermute | solution.py:362
  44.5 0.8 copy-start.4
  45.3 0.8 copy-start.5
  52.9 38.3 %collective-permute-start.20 = (bf16[512,512]{1,0:T(8,128)(2,1)}, bf16[512,512]{1,0:T(8,128)(2,1)S(1)}, u32[]{:S(2)}, u32[]{:S(2)}) collective-permute-start(bf16[512,512]{1,0:T(8,128)(2,1)} %get-tuple-element.62), channel_id=1, source_target_pairs={{0,3},{1,2},{2,1},{3,0},{4,7},{5,6},{6,5},{7,4},{8,11},{9,10},{10,... | collective-permute-start | bytes 1572872 | tf_op jit(solution)/shard_map/ppermute | solution.py:410
  53.9 9.4 %copy-start.14 = (f32[4,136,128]{2,1,0:T(8,128)S(1)}, f32[4,136,128]{2,1,0:T(8,128)}, u32[]{:S(2)}) copy-start(f32[4,136,128]{2,1,0:T(8,128)} %get-tuple-element.45) | copy-start | bytes 835588
  53.9 37.3 %collective-permute-start.21 = (bf16[512,512]{1,0:T(8,128)(2,1)}, bf16[512,512]{1,0:T(8,128)(2,1)S(1)}, u32[]{:S(2)}, u32[]{:S(2)}) collective-permute-start(bf16[512,512]{1,0:T(8,128)(2,1)} %get-tuple-element.63), channel_id=1, source_target_pairs={{0,1},{1,0},{2,3},{3,2},{4,5},{5,4},{6,7},{7,6},{8,9},{9,8},{10,11... | collective-permute-start | bytes 1572872 | tf_op jit(solution)/shard_map/ppermute | solution.py:407
  60.7 21.8 %collective-permute-start.24 = (bf16[512,512]{1,0:T(8,128)(2,1)}, bf16[512,512]{1,0:T(8,128)(2,1)S(1)}, u32[]{:S(2)}, u32[]{:S(2)}) collective-permute-start(bf16[512,512]{1,0:T(8,128)(2,1)} %get-tuple-element.70), channel_id=1, source_target_pairs={{0,3},{1,2},{2,1},{3,0},{4,7},{5,6},{6,5},{7,4},{8,11},{9,10},{10,... | collective-permute-start | bytes 1572872 | tf_op jit(solution)/shard_map/ppermute | solution.py:410
  62.6 21.0 %collective-permute-start.25 = (bf16[512,512]{1,0:T(8,128)(2,1)}, bf16[512,512]{1,0:T(8,128)(2,1)S(1)}, u32[]{:S(2)}, u32[]{:S(2)}) collective-permute-start(bf16[512,512]{1,0:T(8,128)(2,1)} %get-tuple-element.71), channel_id=1, source_target_pairs={{0,1},{1,0},{2,3},{3,2},{4,5},{5,4},{6,7},{7,6},{8,9},{9,8},{10,11... | collective-permute-start | bytes 1572872 | tf_op jit(solution)/shard_map/ppermute | solution.py:407
  63.3 4.5 %collective-permute-start.5 = (f32[2,136,128]{2,1,0:T(8,128)S(1)}, f32[2,136,128]{2,1,0:T(8,128)S(1)}, u32[]{:S(2)}, u32[]{:S(2)}) collective-permute-start(f32[2,136,128]{2,1,0:T(8,128)S(1)} %get-tuple-element.86), channel_id=1, source_target_pairs={{0,4},{4,0},{8,12},{12,8},{16,20},{20,16},{24,28},{28,24},{32,36},... | collective-permute-start | bytes 417800 | tf_op jit(solution)/shard_map/ppermute | solution.py:362
  75.2 6.7 %copy-start.8 = (bf16[512,512]{1,0:T(8,128)(2,1)S(1)}, bf16[512,512]{1,0:T(8,128)(2,1)}, u32[]{:S(2)}) copy-start(bf16[512,512]{1,0:T(8,128)(2,1)} %get-tuple-element.52.xa.a0) | copy-start | bytes 1572868
  75.2 7.3 %copy-start.9 = (bf16[512,512]{1,0:T(8,128)(2,1)S(1)}, bf16[512,512]{1,0:T(8,128)(2,1)}, u32[]{:S(2)}) copy-start(bf16[512,512]{1,0:T(8,128)(2,1)} %get-tuple-element.53.xb.a1) | copy-start | bytes 1572868
  81.9 20.7 %collective-permute-start.14 = (bf16[512,512]{1,0:T(8,128)(2,1)S(1)}, bf16[512,512]{1,0:T(8,128)(2,1)}, u32[]{:S(2)}, u32[]{:S(2)}) collective-permute-start(bf16[512,512]{1,0:T(8,128)(2,1)S(1)} %copy-done.8), channel_id=1, source_target_pairs={{0,1},{1,0},{2,3},{3,2},{4,5},{5,4},{6,7},{7,6},{8,9},{9,8},{10,11... | collective-permute-start | bytes 1572872 | tf_op jit(solution)/shard_map/ppermute | solution.py:407
  82.5 1.1 copy-start.17
  82.5 20.1 %collective-permute-start.15 = (bf16[512,512]{1,0:T(8,128)(2,1)S(1)}, bf16[512,512]{1,0:T(8,128)(2,1)}, u32[]{:S(2)}, u32[]{:S(2)}) collective-permute-start(bf16[512,512]{1,0:T(8,128)(2,1)S(1)} %copy-done.9), channel_id=1, source_target_pairs={{0,3},{1,2},{2,1},{3,0},{4,7},{5,6},{6,5},{7,4},{8,11},{9,10},{10,... | collective-permute-start | bytes 1572872 | tf_op jit(solution)/shard_map/ppermute | solution.py:410
  83.6 0.8 copy-start.18
  91.2 1.0 copy-start.15
  91.2 0.8 copy-start.16
  92.2 7.9 %copy-start.6 = (bf16[512,512]{1,0:T(8,128)(2,1)S(1)}, bf16[512,512]{1,0:T(8,128)(2,1)}, u32[]{:S(2)}) copy-start(bf16[512,512]{1,0:T(8,128)(2,1)} %get-tuple-element.46.xa.a0) | copy-start | bytes 1572868
  92.2 8.3 %copy-start.7 = (bf16[512,512]{1,0:T(8,128)(2,1)S(1)}, bf16[512,512]{1,0:T(8,128)(2,1)}, u32[]{:S(2)}) copy-start(bf16[512,512]{1,0:T(8,128)(2,1)} %get-tuple-element.47.xb.a1) | copy-start | bytes 1572868
  99.1 3.2 %collective-permute-start.26 = (f32[2,136,128]{2,1,0:T(8,128)S(1)}, f32[2,136,128]{2,1,0:T(8,128)S(1)}, u32[]{:S(2)}, u32[]{:S(2)}) collective-permute-start(f32[2,136,128]{2,1,0:T(8,128)S(1)} %dynamic-slice_bitcast_fusion), channel_id=1, source_target_pairs={{0,4},{4,0},{8,12},{12,8},{16,20},{20,16},{24,28},{28,24},{32,36},... | collective-permute-start | bytes 417800 | tf_op jit(solution)/shard_map/ppermute | solution.py:362
  100.1 13.6 %collective-permute-start.6 = (bf16[512,512]{1,0:T(8,128)(2,1)S(1)}, bf16[512,512]{1,0:T(8,128)(2,1)S(1)}, u32[]{:S(2)}, u32[]{:S(2)}) collective-permute-start(bf16[512,512]{1,0:T(8,128)(2,1)S(1)} %copy-done.6), channel_id=1, source_target_pairs={{0,1},{1,0},{2,3},{3,2},{4,5},{5,4},{6,7},{7,6},{8,9},{9,8},{10,11... | collective-permute-start | bytes 1572872 | tf_op jit(solution)/shard_map/ppermute | solution.py:407
  100.5 14.5 %collective-permute-start.7 = (bf16[512,512]{1,0:T(8,128)(2,1)S(1)}, bf16[512,512]{1,0:T(8,128)(2,1)}, u32[]{:S(2)}, u32[]{:S(2)}) collective-permute-start(bf16[512,512]{1,0:T(8,128)(2,1)S(1)} %copy-done.7), channel_id=1, source_target_pairs={{0,3},{1,2},{2,1},{3,0},{4,7},{5,6},{6,5},{7,4},{8,11},{9,10},{10,... | collective-permute-start | bytes 1572872 | tf_op jit(solution)/shard_map/ppermute | solution.py:410
  102.3 7.4 %collective-permute-start.27 = (f32[2,136,128]{2,1,0:T(8,128)S(1)}, f32[2,136,128]{2,1,0:T(8,128)S(1)}, u32[]{:S(2)}, u32[]{:S(2)}) collective-permute-start(f32[2,136,128]{2,1,0:T(8,128)S(1)} %bitcast_add_fusion), channel_id=1, source_target_pairs={{0,32},{4,36},{8,40},{12,44},{16,48},{20,52},{24,56},{28,60},{32,0... | collective-permute-start | bytes 417800 | tf_op jit(solution)/shard_map/ppermute | solution.py:362
  109.1 32.1 %collective-permute-start.17 = (bf16[512,512]{1,0:T(8,128)(2,1)}, bf16[512,512]{1,0:T(8,128)(2,1)S(1)}, u32[]{:S(2)}, u32[]{:S(2)}) collective-permute-start(bf16[512,512]{1,0:T(8,128)(2,1)} %get-tuple-element.57), channel_id=1, source_target_pairs={{0,1},{1,0},{2,3},{3,2},{4,5},{5,4},{6,7},{7,6},{8,9},{9,8},{10,11... | collective-permute-start | bytes 1572872 | tf_op jit(solution)/shard_map/ppermute | solution.py:407
  109.7 31.3 %collective-permute-start.28 = (f32[2,136,128]{2,1,0:T(8,128)S(1)}, f32[2,136,128]{2,1,0:T(8,128)S(1)}, u32[]{:S(2)}, u32[]{:S(2)}) collective-permute-start(f32[2,136,128]{2,1,0:T(8,128)S(1)} %add.140), channel_id=1, source_target_pairs={{0,96},{4,100},{8,104},{12,108},{16,112},{20,116},{24,120},{28,124... | collective-permute-start | bytes 417800 | tf_op jit(solution)/shard_map/ppermute | solution.py:362
  112.6 28.9 %collective-permute-start.16 = (bf16[512,512]{1,0:T(8,128)(2,1)}, bf16[512,512]{1,0:T(8,128)(2,1)S(1)}, u32[]{:S(2)}, u32[]{:S(2)}) collective-permute-start(bf16[512,512]{1,0:T(8,128)(2,1)} %get-tuple-element.55), channel_id=1, source_target_pairs={{0,3},{1,2},{2,1},{3,0},{4,7},{5,6},{6,5},{7,4},{8,11},{9,10},{10,... | collective-permute-start | bytes 1572872 | tf_op jit(solution)/shard_map/ppermute | solution.py:410
  113.7 1.3 copy-start.19
  121.5 20.9 %collective-permute-start.13 = (bf16[512,512]{1,0:T(8,128)(2,1)}, bf16[512,512]{1,0:T(8,128)(2,1)S(1)}, u32[]{:S(2)}, u32[]{:S(2)}) collective-permute-start(bf16[512,512]{1,0:T(8,128)(2,1)} %get-tuple-element.51), channel_id=1, source_target_pairs={{0,1},{1,0},{2,3},{3,2},{4,5},{5,4},{6,7},{7,6},{8,9},{9,8},{10,11... | collective-permute-start | bytes 1572872 | tf_op jit(solution)/shard_map/ppermute | solution.py:407
  121.6 28.1 %collective-permute-start.12 = (bf16[512,512]{1,0:T(8,128)(2,1)}, bf16[512,512]{1,0:T(8,128)(2,1)S(1)}, u32[]{:S(2)}, u32[]{:S(2)}) collective-permute-start(bf16[512,512]{1,0:T(8,128)(2,1)} %get-tuple-element.49), channel_id=1, source_target_pairs={{0,3},{1,2},{2,1},{3,0},{4,7},{5,6},{6,5},{7,4},{8,11},{9,10},{10,... | collective-permute-start | bytes 1572872 | tf_op jit(solution)/shard_map/ppermute | solution.py:410
  132.2 9.0 %copy-start.11 = (f32[512,512]{1,0:T(8,128)S(1)}, f32[512,512]{1,0:T(8,128)}, u32[]{:S(2)}) copy-start(f32[512,512]{1,0:T(8,128)} %get-tuple-element.56) | copy-start | bytes 3145732
  141.1 1.2 copy-start.10
  141.1 6.4 %collective-permute-start.29 = (f32[2,2,136,128]{3,2,1,0:T(8,128)S(1)}, f32[2,2,136,128]{3,2,1,0:T(8,128)S(1)}, u32[]{:S(2)}, u32[]{:S(2)}) collective-permute-start(f32[2,2,136,128]{3,2,1,0:T(8,128)S(1)} %pad_maximum_fusion.3), channel_id=1, source_target_pairs={{0,8},{4,12},{8,0},{12,4},{16,24},{20,28},{24,16},{28,20},{32,40},... | collective-permute-start | bytes 835592 | tf_op jit(solution)/shard_map/ppermute | solution.py:362
  141.3 1.4 copy-start.13
  142.3 7.5 %copy-start.12 = (f32[512,512]{1,0:T(8,128)S(1)}, f32[512,512]{1,0:T(8,128)}, u32[]{:S(2)}) copy-start(f32[512,512]{1,0:T(8,128)} %get-tuple-element.48) | copy-start | bytes 3145732
  147.6 5.2 %collective-permute-start.30 = (f32[2,136,128]{2,1,0:T(8,128)S(1)}, f32[2,136,128]{2,1,0:T(8,128)S(1)}, u32[]{:S(2)}, u32[]{:S(2)}) collective-permute-start(f32[2,136,128]{2,1,0:T(8,128)S(1)} %select_add_fusion.1), channel_id=1, source_target_pairs={{0,24},{4,28},{8,16},{12,20},{16,8},{20,12},{24,0},{28,4},{32,56},... | collective-permute-start | bytes 417800 | tf_op jit(solution)/shard_map/ppermute | solution.py:362
  152.8 5.5 %collective-permute-start.31 = (f32[2,136,128]{2,1,0:T(8,128)S(1)}, f32[2,136,128]{2,1,0:T(8,128)S(1)}, u32[]{:S(2)}, u32[]{:S(2)}) collective-permute-start(f32[2,136,128]{2,1,0:T(8,128)S(1)} %get-tuple-element.84), channel_id=1, source_target_pairs={{0,4},{4,0},{8,12},{12,8},{16,20},{20,16},{24,28},{28,24},{32,36},... | collective-permute-start | bytes 417800 | tf_op jit(solution)/shard_map/ppermute | solution.py:362
